TPU v7x, 128 devices: a whole 4x4x4 slice. The times are simulated.
128 devices in a mesh: segment: 4 (over z_lo, core), lon: 8 (over z_hi, y), lat: 4 (over x).
Axes of the slice: x: 4, y: 4, z: 4 (z_hi: 2, z_lo: 2; z = z_hi * 2 + z_lo), core: 2. Of those that a mesh axis runs over, the one named last changes fastest.
Arguments:
- latents: bfloat16 [4, 2, 24, 192, 512], P(None, None, 'lat', 'lon'), may hold values from -6 to 6
- segment_depth: int32 [4], replicated, may hold values from 1 to 2, as said below
- shift_flags: int32 [8, 2], P('segment'), may hold values from 0 to 1
- w_qkv: bfloat16 [8, 512, 1536], P('segment'), may hold values from -0.25 to 0.25
- w_out: bfloat16 [8, 512, 512], P('segment'), may hold values from -0.25 to 0.25
- w_up: bfloat16 [8, 512, 2048], P('segment'), may hold values from -0.25 to 0.25
- w_down: bfloat16 [8, 2048, 512], P('segment'), may hold values from -0.125 to 0.125
- gains: float32 [8, 2, 512], P('segment'), may hold values from 0.25 to 1.75
- logit_scale: float32 [8, 8], P('segment'), may hold values from 2 to 100
Outputs:
- sections: float32 [4, 4, 2, 24, 192, 512], P('segment', None, None, 'lat', 'lon')
Inputs may be any that keep to these rules, and one draw needn't show every extreme that they name: `segment_depth`: at least one section applies 2 layers and at least one applies a single layer.
All inputs are finite; a program needn't handle non-finite values.
Results may differ from a plain program's by a relative error of at most 0.035.
The roundings to bfloat16 on the way count: a program that leaves them out, or rounds other values in their place, can miss the bound.
Values may be sent and summed in bfloat16 or wider, within the bound.
A program may use at most 192 MiB of HBM per device.

v0:
```python
import functools

import jax
import jax.numpy as jnp
import numpy as np
from jax import lax
from jax.experimental import pallas as pl
from jax.experimental.pallas import tpu as pltpu
from jax.sharding import PartitionSpec as P

MESH = pl.DeviceIdType.MESH
HALF = 144
CELLS = 2 * HALF
PART = HALF // 2
REACH = 80
EDGE = 48
AT_LAT = CELLS
AT_LON = AT_LAT + 2 * REACH
AT_BOTH = AT_LON + 2 * EDGE
WIDE = AT_BOTH + EDGE
SLOTS = 4
LENGTHS = ((3, 3), (4, 3), (3, 4))
LOG2E = 1.4426950408889634
BIG = 1e30


def moves():
    table = np.zeros((CELLS, 128), np.float32)
    for core in range(2):
        far_half = 1 - core
        for lat in range(2):
            for lon in range(2):
                which = core * 8 + lat * 2 + lon
                for at in range(CELLS):
                    window, half, pair, cell = at // 144, at % 144 // 72, at % 72 // 36, at % 36
                    level, row, column = cell // 18, cell % 18 // 6, cell % 6
                    column += (2 * window + pair) * 6 + lon * (6 - 12 * core)
                    across = column >= 24 or column < 0
                    edge_column = column - 24 if core == 0 else column + 24 - 16
                    along = lat == 1 and half == far_half
                    source = 1 - half if lat else half
                    edge = (level * 3 + row) * 8 + edge_column
                    if along and across:
                        take = AT_BOTH + edge
                    elif along:
                        take = AT_LAT + level * REACH + core * 8 + row * 24 + column
                    elif across:
                        take = AT_LON + source * EDGE + edge
                    else:
                        take = level * 144 + (source * 3 + row) * 24 + column
                    table[at, which] = take

                    level, row, column = at // 144, at % 144 // 24, at % 24
                    half, row = row // 3, row % 3
                    along = lat == 1 and half == core
                    source = 1 - half if lat else half
                    column -= lon * (6 - 12 * core)
                    across = column >= 24 or column < 0
                    column %= 24
                    window, pair = column // 12, column % 12 // 6
                    inside = source * 72 + pair * 36 + level * 18 + row * 6 + column % 6
                    if along and across:
                        take = AT_BOTH + inside - (0 if core else 96)
                    elif along:
                        take = AT_LAT + window * REACH + inside - (0 if core else 64)
                    elif across:
                        take = AT_LON + source * EDGE + inside - source * 64 - (0 if core else 32)
                    else:
                        take = window * 144 + inside
                    table[at, which + 4] = take
    return table


def normed(values, gain):
    mean = jnp.mean(values, axis=-1, keepdims=True)
    centred = values - mean
    var = jnp.mean(centred * centred, axis=-1, keepdims=True)
    return centred * lax.rsqrt(var + 1e-05) * gain


def gelu(u):
    inner = u * (0.7978845608028654 + 0.035677408136300125 * (u * u))
    half = 0.5 * u
    return half + half * jnp.tanh(inner)


def dot(a, b):
    return jnp.dot(a, b, preferred_element_type=jnp.float32)


def kernel(
    lon_n, lat_n, lengths, depth_ref, latents, small_in, gains_in, table, w_qkv, w_out, w_up, w_down, sections,
    wq_a, wo_a, wu_a, wd_a, wq_b, wo_b, wu_b, wd_b, small, gains, fwd, bwd, x, src, packed, ret, stage, hand_out, hand_in, cross, ones,
    w_recv, w_send, p_recv, p_send, f_recv, f_send, b_recv, b_send, in_sem, h_recv, h_send,
    o_recv, o_send,
):
    seg = lax.axis_index("segment")
    lon = lax.axis_index("lon")
    lat = lax.axis_index("lat")
    chip = seg // 2
    core = lax.rem(seg, 2)
    mate_core = 1 - core
    north, south = lax.rem(lat + lat_n - 1, lat_n), lax.rem(lat + 1, lat_n)
    west, east = lax.rem(lon + lon_n - 1, lon_n), lax.rem(lon + 1, lon_n)

    def device(s, o, a):
        return {"segment": s, "lon": o, "lat": a}

    out_lat, home_lat = north + core * (south - north), south + core * (north - south)
    out_lon, home_lon = west + core * (east - west), east + core * (west - east)
    to_n, to_s = device(seg, lon, out_lat), device(seg, lon, home_lat)
    to_w, to_e = device(seg, out_lon, lat), device(seg, home_lon, lat)
    to_nw, to_se = device(seg, out_lon, out_lat), device(seg, home_lon, home_lat)
    mate = device(chip * 2 + mate_core, lon, lat)
    other = device(lax.rem(seg + 2, 4), lon, lat)

    steps = lengths[0] + chip * (lengths[1] - lengths[0])
    depth = depth_ref[2 * chip]
    layers = depth + depth_ref[2 * chip + 1]

    first_weights = (wq_a, wo_a, wu_a, wd_a)
    later_weights = (wq_b, wo_b, wu_b, wd_b)
    held_weights = (w_qkv, w_out, w_up, w_down)

    def each_weight(i, k, act):
        if i == 1:
            act(held_weights[k].at[1], later_weights[k].at[2 * core])
            return

        @pl.when(core == 0)
        def _():
            act(held_weights[k].at[0], first_weights[k])

        @pl.when(core == 1)
        def _():
            act(held_weights[k].at[0], later_weights[k].at[1])

    def own_weights(i, k):
        slot = core * 2 + i
        each_weight(
            i, k,
            lambda held, kept: pltpu.make_async_copy(held, kept, w_recv.at[slot, k]).start(),
        )

    def lent_weights(i, k, act):
        slot = core * 2 + i
        each_weight(
            i, k,
            lambda held, kept: act(
                pltpu.make_async_remote_copy(
                    src_ref=held, dst_ref=kept, send_sem=w_send.at[i, k],
                    recv_sem=w_recv.at[slot, k], device_id=mate, device_id_type=MESH,
                )
            ),
        )

    def weights_here(slot, k):
        kept = first_weights[k] if slot == 0 else later_weights[k].at[slot - 1]
        pltpu.make_async_copy(held_weights[k].at[0], kept, w_recv.at[slot, k]).wait()

    tiny = ((small_in, small), (gains_in, gains))

    def own_params(k):
        held, kept = tiny[k]
        return pltpu.make_async_copy(held, kept.at[pl.ds(core * 2, 2)], p_recv.at[core, k])

    def lent_params(k):
        held, kept = tiny[k]
        return pltpu.make_async_remote_copy(
            src_ref=held, dst_ref=kept.at[pl.ds(core * 2, 2)], send_sem=p_send.at[k],
            recv_sem=p_recv.at[core, k], device_id=mate, device_id_type=MESH,
        )

    def edges(pieces, send, recv):
        return [
            pltpu.make_async_remote_copy(
                src_ref=source, dst_ref=target, send_sem=send.at[i], recv_sem=recv.at[i],
                device_id=to, device_id_type=MESH,
            )
            for i, (source, target, to) in enumerate(pieces)
        ]

    def rows_from(start, size):
        return pl.ds(pl.multiple_of(start, 16), size)

    def forth(b):
        return edges(
            (
                (src.at[b, rows_from(64 * core, REACH)], src.at[b, pl.ds(AT_LAT, REACH)], to_n),
                (
                    src.at[b, rows_from(HALF + 64 * core, REACH)],
                    src.at[b, pl.ds(AT_LAT + REACH, REACH)], to_n,
                ),
                (packed.at[b], src.at[b, pl.ds(AT_LON, 2 * EDGE)], to_w),
                (packed.at[b, rows_from(EDGE * core, EDGE)], src.at[b, pl.ds(AT_BOTH, EDGE)], to_nw),
            ),
            f_send.at[b], f_recv.at[b],
        )

    def back(b):
        return edges(
            (
                (ret.at[b, rows_from(64 - 64 * core, REACH)], ret.at[b, pl.ds(AT_LAT, REACH)], to_s),
                (
                    ret.at[b, rows_from(208 - 64 * core, REACH)],
                    ret.at[b, pl.ds(AT_LAT + REACH, REACH)], to_s,
                ),
                (ret.at[b, rows_from(176 - 176 * core, EDGE)], ret.at[b, pl.ds(AT_LON, EDGE)], to_e),
                (
                    ret.at[b, rows_from(240 - 176 * core, EDGE)],
                    ret.at[b, pl.ds(AT_LON + EDGE, EDGE)], to_e,
                ),
                (ret.at[b, rows_from(240 - 240 * core, EDGE)], ret.at[b, pl.ds(AT_BOTH, EDGE)], to_se),
            ),
            b_send.at[b], b_recv.at[b],
        )

    def edge_of(values, column):
        rows = [
            level * 144 + row * 24 + column
            for half in ((0, 1, 2), (3, 4, 5)) for level in (0, 1) for row in half
        ]
        return jnp.concatenate([values[r : r + 8] for r in rows], axis=0)

    def far_edge(values):
        return jnp.where(core == 0, edge_of(values, 0), edge_of(values, 16)).astype(jnp.bfloat16)

    def load_input(b):
        return pltpu.make_async_copy(
            latents.at[core + 2 * b], src.at[b, pl.ds(0, CELLS)], in_sem.at[b]
        )

    def hand_on(b):
        return pltpu.make_async_remote_copy(
            src_ref=hand_out.at[b], dst_ref=hand_in.at[b], send_sem=h_send.at[b],
            recv_sem=h_recv.at[b], device_id=other, device_id_type=MESH,
        )

    def keep_output(b, s):
        return pltpu.make_async_copy(
            stage.at[b, s], sections.at[core + 2 * b], o_recv.at[b, 0]
        )

    def give_output(b, s):
        return pltpu.make_async_remote_copy(
            src_ref=stage.at[b, s], dst_ref=sections.at[core + 2 * b], send_sem=o_send.at[b],
            recv_sem=o_recv.at[b, 1], device_id=mate, device_id_type=MESH,
        )

    barrier = pltpu.get_barrier_semaphore()
    for k in range(4):
        own_weights(0, k)
    for k in range(2):
        own_params(k).start()

    @pl.when(chip == 0)
    def _():
        for b in range(2):
            load_input(b).start()

    for to in (to_n, to_s, to_w, to_e, to_nw, to_se, mate, other):
        pl.semaphore_signal(barrier, inc=1, device_id=to, device_id_type=MESH)
    pl.semaphore_wait(barrier, 8)

    for k in range(2):
        lent_params(k).start()
    for i in range(2):
        for k in range(4):
            lent_weights(i, k, lambda copy: copy.start())
            if i == 1:
                own_weights(i, k)

    @pl.when(chip == 0)
    def _():
        for b in range(2):
            load_input(b).wait()
            entry = src[b, 0:CELLS].astype(jnp.float32)
            x[b] = entry
            packed[b] = far_edge(entry)
            for copy in forth(b):
                copy.start()

    @pl.when(chip == 1)
    def _():
        for b in range(2):
            hand_on(b).wait_recv()
            src[b, 0:CELLS] = hand_in[b]
            entry = hand_in[b].astype(jnp.float32)
            x[b] = entry
            packed[b] = far_edge(entry)
            for copy in forth(b):
                copy.start()

    for k, (held, kept) in enumerate(tiny):
        own_params(k).wait()
        pltpu.make_async_copy(
            held, kept.at[pl.ds(mate_core * 2, 2)], p_recv.at[mate_core, k]
        ).wait()

    rows = lax.broadcasted_iota(jnp.int32, (HALF, HALF), 0)
    cols = lax.broadcasted_iota(jnp.int32, (HALF, HALF), 1)
    split = (rows < PART) != (cols < PART)
    is_last = jnp.where(lat == (lat_n - 1) * (1 - core), 1.0, 0.0)
    cross[...] = jnp.where(split, -BIG, 0.0) * is_last
    r256 = lax.broadcasted_iota(jnp.int32, (256, 256), 0)
    c256 = lax.broadcasted_iota(jnp.int32, (256, 256), 1)
    ones[...] = jnp.where(r256 // 64 == c256 // 64, 1.0, 0.0).astype(jnp.bfloat16)

    place = lax.broadcasted_iota(jnp.int32, (CELLS, WIDE), 1).astype(jnp.float32)

    def slot_of(step):
        return jnp.clip(step + jnp.where(step == 0, 0, 2 - depth), 0, SLOTS - 1)

    def choose(step, carry):
        f_lat = small[slot_of(step), 0:1, 0:1]
        f_lon = small[slot_of(step), 0:1, 1:2]
        picks = (
            (1.0 - f_lat) * (1.0 - f_lon), (1.0 - f_lat) * f_lon,
            f_lat * (1.0 - f_lon), f_lat * f_lon,
        )
        for first, kept in ((0, fwd), (4, bwd)):
            at = sum(
                jnp.where(
                    core == 0, table[:, first + i : first + i + 1],
                    table[:, first + i + 8 : first + i + 9],
                ) * picks[i]
                for i in range(4)
            )
            kept[step] = jnp.where(place == at, 1.0, 0.0).astype(jnp.bfloat16)
        return carry

    lax.fori_loop(0, steps, choose, 0)

    lane = lax.broadcasted_iota(jnp.int32, (1, 256), 1)
    masks = [jnp.where(lane // 64 == h, 1.0, 0.0).astype(jnp.bfloat16) for h in range(4)]
    first_of_pair = lax.broadcasted_iota(jnp.int32, (HALF, 128), 1) < 64

    def unit(block):
        total = dot((block * block).astype(jnp.bfloat16), ones[...])
        return (block * lax.rsqrt(total + 1e-06)).astype(jnp.bfloat16)

    def attend(b, step, l, weight):
        for copy in forth(b):
            copy.wait()
        cells = dot(fwd[step], src[b]).astype(jnp.bfloat16)
        bias = small[l, 0:1, 0:1] * cross[...]
        done = [[], []]
        for g in range(2):
            lanes = [slice(p * 512 + g * 256, p * 512 + g * 256 + 256) for p in range(3)]
            q = unit(dot(cells, weight(0, lanes[0])))
            k = unit(dot(cells, weight(0, lanes[1])))
            v = dot(cells, weight(0, lanes[2])).astype(jnp.bfloat16)
            for w in range(2):
                part = slice(w * HALF, w * HALF + HALF)
                heads = jnp.concatenate([q[part] * masks[h] for h in range(4)], axis=0)
                scores = lax.dot_general(
                    heads, k[part], (((1,), (1,)), ((), ())), preferred_element_type=jnp.float32
                )
                expos, shares = [], []
                for h in range(4):
                    scale = small[l, 0:1, 2 + g * 4 + h : 3 + g * 4 + h]
                    score = scores[h * HALF : h * HALF + HALF] * scale + bias
                    expo = jnp.exp2(score - jnp.max(score, axis=-1, keepdims=True))
                    shares.append(1.0 / jnp.sum(expo, axis=-1, keepdims=True))
                    expos.append(expo.astype(jnp.bfloat16))
                mixed = dot(jnp.concatenate(expos, axis=0), v[part])
                for p in range(2):
                    at = slice(p * 128, p * 128 + 128)
                    one = mixed[2 * p * HALF : (2 * p + 1) * HALF, at] * shares[2 * p]
                    two = mixed[(2 * p + 1) * HALF : (2 * p + 2) * HALF, at] * shares[2 * p + 1]
                    done[w].append(jnp.where(first_of_pair, one, two).astype(jnp.bfloat16))
        for w in range(2):
            ret[b, w * HALF : w * HALF + HALF] = jnp.concatenate(done[w], axis=1)
        for copy in back(b):
            copy.start()

    def feed(b, step, l, weight):
        for copy in back(b):
            copy.wait()
        mixed = dot(bwd[step], ret[b]).astype(jnp.bfloat16)
        state = x[b]
        first = state + normed(dot(mixed, weight(1)), gains[l, 0:1])
        firstb = first.astype(jnp.bfloat16)
        hidden = jnp.concatenate(
            [
                gelu(dot(firstb, weight(2, slice(c, c + 256)))).astype(jnp.bfloat16)
                for c in range(0, 2048, 256)
            ],
            axis=1,
        )
        fresh = first + normed(dot(hidden, weight(3)), gains[l, 1:2])
        fresh = jnp.where(step < layers, fresh, state)
        x[b] = fresh

        @pl.when(step < steps - 1)
        def _():
            src[b, 0:CELLS] = fresh.astype(jnp.bfloat16)
            packed[b] = far_edge(fresh)
            for copy in forth(b):
                copy.start()

        def emit(s, value):
            stage[b, s] = value

            @pl.when(s == core)
            def _():
                keep_output(b, s).start()

            @pl.when(s != core)
            def _():
                give_output(b, s).start()

        @pl.when(step == 1)
        def _():
            emit(0, jnp.where(depth == 1, state, fresh))

        @pl.when(step == steps - 1)
        def _():
            emit(1, fresh)

            @pl.when(chip == 0)
            def _():
                hand_out[b] = fresh.astype(jnp.bfloat16)
                hand_on(b).start()

    def layer(step, l, weight):
        def one(b, c):
            attend(b, step, l, weight)
            return c

        def two(b, c):
            feed(b, step, l, weight)
            return c

        return one, two

    def weight_a(k, lanes=slice(None)):
        return first_weights[k][:, lanes]

    weights_here(0, 0)
    one, two = layer(0, 0, weight_a)
    lax.fori_loop(0, 2, one, 0)
    for k in range(1, 4):
        weights_here(0, k)
    lax.fori_loop(0, 2, two, 0)

    for slot in range(1, SLOTS):
        for k in range(4):
            weights_here(slot, k)

    def later(step, carry):
        l = slot_of(step)

        def weight_b(k, lanes=slice(None)):
            return later_weights[k][jnp.maximum(l, 1) - 1, :, lanes]

        one, two = layer(step, l, weight_b)
        lax.fori_loop(0, 2, one, 0)
        lax.fori_loop(0, 2, two, 0)
        return carry

    lax.fori_loop(1, steps, later, 0)

    for i in range(2):
        for k in range(4):
            lent_weights(i, k, lambda copy: copy.wait_send())
    for k in range(2):
        lent_params(k).wait_send()

    @pl.when(chip == 0)
    def _():
        for b in range(2):
            hand_on(b).wait_send()

    for b in range(2):
        keep_output(b, core).wait()
        give_output(b, mate_core).wait()


def shards(latents, segment_depth, shift_flags, w_qkv, w_out, w_up, w_down, gains, logit_scale,
           lon_n, lat_n):
    micro, levels, clat, clon, width = latents.shape
    cells = latents.reshape(micro, CELLS, width)
    small = jnp.concatenate(
        [shift_flags.astype(jnp.float32), logit_scale * LOG2E, jnp.zeros((2, 118), jnp.float32)],
        axis=1,
    ).reshape(2, 1, 128)
    table = jnp.asarray(moves())
    hbm = pl.BlockSpec(memory_space=pl.ANY)
    bf16, f32 = jnp.bfloat16, jnp.float32
    dma = pltpu.SemaphoreType.DMA
    def run(which):
        lengths = LENGTHS[which]
        return pl.pallas_call(
            functools.partial(kernel, lon_n, lat_n, lengths),
            out_shape=jax.ShapeDtypeStruct((micro, CELLS, width), f32),
            in_specs=[
                pl.BlockSpec(memory_space=pltpu.SMEM), hbm, hbm, hbm,
                pl.BlockSpec(memory_space=pltpu.VMEM), hbm, hbm, hbm, hbm,
            ],
            out_specs=hbm,
            scratch_shapes=[
                pltpu.VMEM((width, 3 * width), bf16),
                pltpu.VMEM((width, width), bf16),
                pltpu.VMEM((width, 4 * width), bf16),
                pltpu.VMEM((4 * width, width), bf16),
                pltpu.VMEM((SLOTS - 1, width, 3 * width), bf16),
                pltpu.VMEM((SLOTS - 1, width, width), bf16),
                pltpu.VMEM((SLOTS - 1, width, 4 * width), bf16),
                pltpu.VMEM((SLOTS - 1, 4 * width, width), bf16),
                pltpu.VMEM((SLOTS, 1, 128), f32),
                pltpu.VMEM((SLOTS, 2, width), f32),
                pltpu.VMEM((SLOTS, CELLS, WIDE), bf16),
                pltpu.VMEM((SLOTS, CELLS, WIDE), bf16),
                pltpu.VMEM((2, CELLS, width), f32),
                pltpu.VMEM((2, WIDE, width), bf16),
                pltpu.VMEM((2, 2 * EDGE, width), bf16),
                pltpu.VMEM((2, WIDE, width), bf16),
                pltpu.VMEM((2, 2, CELLS, width), f32),
                pltpu.VMEM((2, CELLS, width), bf16),
                pltpu.VMEM((2, CELLS, width), bf16),
                pltpu.VMEM((HALF, HALF), f32),
                pltpu.VMEM((256, 256), bf16),
                dma((SLOTS, 4)), dma((2, 4)), dma((2, 2)), dma((2,)),
                dma((2, 4)), dma((2, 4)), dma((2, 5)), dma((2, 5)),
                dma((2,)), dma((2,)), dma((2,)), dma((2, 2)), dma((2,)),
            ],
            compiler_params=pltpu.CompilerParams(
                collective_id=which, has_side_effects=True, vmem_limit_bytes=60 * 1024 * 1024
            ),
            cost_estimate=pl.CostEstimate(
                flops=16 * 2 * 10**9, bytes_accessed=20 * 10**6, transcendentals=10**7
            ),
        )

    operands = (segment_depth, cells, small, gains, table, w_qkv, w_out, w_up, w_down)
    lengths = segment_depth[0:2].sum(), segment_depth[2:4].sum()
    out = lax.switch(
        lengths[0] // 4 + 2 * (lengths[1] // 4),
        [run(which) for which in range(len(LENGTHS))],
        *operands,
    )
    return out.reshape(1, micro, levels, clat, clon, width)


def solution(mesh):
    placed = (
        P(None, None, "lat", "lon", None),
        P(),
        P("segment", None),
        P("segment", None, None),
        P("segment", None, None),
        P("segment", None, None),
        P("segment", None, None),
        P("segment", None, None),
        P("segment", None),
    )
    return jax.shard_map(
        functools.partial(shards, lon_n=mesh.shape["lon"], lat_n=mesh.shape["lat"]),
        mesh=mesh,
        in_specs=placed,
        out_specs=P("segment", None, None, "lat", "lon", None),
        check_vma=False,
    )
```

profile of v0, /device:TPU:33, one launch (start us, length us, event | category | flops | bytes accessed | tf_op | source)
XLA Modules:
  0.0 163.9 jit_solution(5374164434069619774)
XLA Ops:
  0.0 0.1 pad.2.clone
  0.1 0.7 convert_element_type.3
  0.8 0.7 broadcast_multiply_fusion
  1.4 0.1 maximum_maximum_fusion
  1.5 1.5 slice_reduce_fusion
  8.4 154.1 %conditional.1 = (f32[1,4,2,6,24,512]{5,4,3,2,1,0:T(8,128)S(1)}) conditional(s32[]{:T(128)} %clamp.3, (s32[4]{0:T(128)}, bf16[4,2,6,24,512]{4,3,2,1,0:T(8,128)(2,1)}, f32[2,128]{1,0:T(2,128)S(1)}, f32[2,2,512]{2,1,0:T(2,128)}, bf16[2,512,1536]{2,1,0:T(8,128)(2,1)}, /*index=5*/bf16[2,512,512]{2,1,0:T(8,128)(2,1)}, ...), branch_computations={%region_2.3_spmd.clone, %region_3.4_spmd.clone, %region_4.5_spmd.c... | conditional | flops 32000000000 | bytes 20000008 | solution.py:538
  8.4 153.8 %branch_0_fun.1 = f32[4,288,512]{2,1,0:T(8,128)S(1)} custom-call(s32[4]{0:T(128)} %get-tuple-element.140.depth_ref, bf16[4,288,512]{2,1,0:T(8,128)(2,1)} %bitcast.15, f32[2,1,128]{2,1,0:T(1,128)S(1)} %bitcast.12, f32[2,2,512]{2,1,0:T(2,128)} %get-tuple-element.142.gains_in, f32[288,128]{1,0:T(8,128)} %constant.31.clone.4.table, ...), custom_call_target="tpu_custom_call" | custom-call | flops 32000000000 | bytes 20000000 | tf_op jit(solution)/shard_map/cond/branch_0_fun/pallas_call | solution.py:538
  162.5 1.4 copy.63
  (1 shorter events, 0.0 us)
where the time goes:
time: 164 us
  Pallas kernels  154 us (94%)
  between operations  5.39 us (3%)
  other arithmetic  2.96 us (2%)
    pallas_call x1, Pallas kernels, shards(): lax.switch(lengths[0] // 4 + 2 * (lengths[1] // 4), [run(which) for which...  154 us

commit v1 on v0

--- a/solution.py
+++ b/solution.py
@@ -14,10 +14,11 @@
 PART = HALF // 2
 REACH = 80
 EDGE = 48
-AT_LAT = CELLS
-AT_LON = AT_LAT + 2 * REACH
+AT_LON = CELLS
 AT_BOTH = AT_LON + 2 * EDGE
-WIDE = AT_BOTH + EDGE
+TAKEN = AT_BOTH + EDGE
+AT_LAT = TAKEN
+WIDE = AT_LAT + 2 * REACH
 SLOTS = 4
 LENGTHS = ((3, 3), (4, 3), (3, 4))
 LOG2E = 1.4426950408889634
@@ -42,8 +43,6 @@
                     edge = (level * 3 + row) * 8 + edge_column
                     if along and across:
                         take = AT_BOTH + edge
-                    elif along:
-                        take = AT_LAT + level * REACH + core * 8 + row * 24 + column
                     elif across:
                         take = AT_LON + source * EDGE + edge
                     else:
@@ -61,8 +60,6 @@
                     inside = source * 72 + pair * 36 + level * 18 + row * 6 + column % 6
                     if along and across:
                         take = AT_BOTH + inside - (0 if core else 96)
-                    elif along:
-                        take = AT_LAT + window * REACH + inside - (0 if core else 64)
                     elif across:
                         take = AT_LON + source * EDGE + inside - source * 64 - (0 if core else 32)
                     else:
@@ -71,17 +68,16 @@
     return table
 
 
-def normed(values, gain):
+def normed(values, gain, eps):
     mean = jnp.mean(values, axis=-1, keepdims=True)
     centred = values - mean
     var = jnp.mean(centred * centred, axis=-1, keepdims=True)
-    return centred * lax.rsqrt(var + 1e-05) * gain
-
-
-def gelu(u):
+    return centred * lax.rsqrt(var + eps) * gain
+
+
+def twice_gelu(u):
     inner = u * (0.7978845608028654 + 0.035677408136300125 * (u * u))
-    half = 0.5 * u
-    return half + half * jnp.tanh(inner)
+    return u + u * jnp.tanh(inner)
 
 
 def dot(a, b):
@@ -264,11 +260,8 @@
 
     for k in range(2):
         lent_params(k).start()
-    for i in range(2):
-        for k in range(4):
-            lent_weights(i, k, lambda copy: copy.start())
-            if i == 1:
-                own_weights(i, k)
+    for k in range(4):
+        lent_weights(0, k, lambda copy: copy.start())
 
     @pl.when(chip == 0)
     def _():
@@ -306,7 +299,7 @@
     c256 = lax.broadcasted_iota(jnp.int32, (256, 256), 1)
     ones[...] = jnp.where(r256 // 64 == c256 // 64, 1.0, 0.0).astype(jnp.bfloat16)
 
-    place = lax.broadcasted_iota(jnp.int32, (CELLS, WIDE), 1).astype(jnp.float32)
+    place = lax.broadcasted_iota(jnp.int32, (CELLS, TAKEN), 1).astype(jnp.float32)
 
     def slot_of(step):
         return jnp.clip(step + jnp.where(step == 0, 0, 2 - depth), 0, SLOTS - 1)
@@ -339,10 +332,23 @@
         total = dot((block * block).astype(jnp.bfloat16), ones[...])
         return (block * lax.rsqrt(total + 1e-06)).astype(jnp.bfloat16)
 
+    reach_row = lax.broadcasted_iota(jnp.int32, (REACH, 1), 0)
+
+    def replace_rows(buf, b, l, far):
+        kept = (reach_row >= 8 * far) & (reach_row < PART + 8 * far)
+        theirs = jnp.where(kept, small[l, 0:1, 0:1], 0.0)
+        ours = (1.0 - theirs).astype(jnp.bfloat16)
+        theirs = theirs.astype(jnp.bfloat16)
+        for i in range(2):
+            at = rows_from(i * HALF + 64 * far, REACH)
+            came = buf[b, AT_LAT + i * REACH : AT_LAT + (i + 1) * REACH]
+            buf[b, at] = buf[b, at] * ours + came * theirs
+
     def attend(b, step, l, weight):
         for copy in forth(b):
             copy.wait()
-        cells = dot(fwd[step], src[b]).astype(jnp.bfloat16)
+        replace_rows(src, b, l, core)
+        cells = dot(fwd[step], src[b, 0:TAKEN]).astype(jnp.bfloat16)
         bias = small[l, 0:1, 0:1] * cross[...]
         done = [[], []]
         for g in range(2):
@@ -361,7 +367,9 @@
                     scale = small[l, 0:1, 2 + g * 4 + h : 3 + g * 4 + h]
                     score = scores[h * HALF : h * HALF + HALF] * scale + bias
                     expo = jnp.exp2(score - jnp.max(score, axis=-1, keepdims=True))
-                    shares.append(1.0 / jnp.sum(expo, axis=-1, keepdims=True))
+                    total = jnp.sum(expo, axis=-1, keepdims=True)
+                    share = pl.reciprocal(total, approx=True)
+                    shares.append(share * (2.0 - total * share))
                     expos.append(expo.astype(jnp.bfloat16))
                 mixed = dot(jnp.concatenate(expos, axis=0), v[part])
                 for p in range(2):
@@ -377,18 +385,19 @@
     def feed(b, step, l, weight):
         for copy in back(b):
             copy.wait()
-        mixed = dot(bwd[step], ret[b]).astype(jnp.bfloat16)
+        replace_rows(ret, b, l, 1 - core)
+        mixed = dot(bwd[step], ret[b, 0:TAKEN]).astype(jnp.bfloat16)
         state = x[b]
-        first = state + normed(dot(mixed, weight(1)), gains[l, 0:1])
+        first = state + normed(dot(mixed, weight(1)), gains[l, 0:1], 1e-05)
         firstb = first.astype(jnp.bfloat16)
         hidden = jnp.concatenate(
             [
-                gelu(dot(firstb, weight(2, slice(c, c + 256)))).astype(jnp.bfloat16)
+                twice_gelu(dot(firstb, weight(2, slice(c, c + 256)))).astype(jnp.bfloat16)
                 for c in range(0, 2048, 256)
             ],
             axis=1,
         )
-        fresh = first + normed(dot(hidden, weight(3)), gains[l, 1:2])
+        fresh = first + normed(dot(hidden, weight(3)), gains[l, 1:2], 4e-05)
         fresh = jnp.where(step < layers, fresh, state)
         x[b] = fresh
 
@@ -442,6 +451,9 @@
     lax.fori_loop(0, 2, one, 0)
     for k in range(1, 4):
         weights_here(0, k)
+    for k in range(4):
+        lent_weights(1, k, lambda copy: copy.start())
+        own_weights(1, k)
     lax.fori_loop(0, 2, two, 0)
 
     for slot in range(1, SLOTS):
@@ -510,8 +522,8 @@
                 pltpu.VMEM((SLOTS - 1, 4 * width, width), bf16),
                 pltpu.VMEM((SLOTS, 1, 128), f32),
                 pltpu.VMEM((SLOTS, 2, width), f32),
-                pltpu.VMEM((SLOTS, CELLS, WIDE), bf16),
-                pltpu.VMEM((SLOTS, CELLS, WIDE), bf16),
+                pltpu.VMEM((SLOTS, CELLS, TAKEN), bf16),
+                pltpu.VMEM((SLOTS, CELLS, TAKEN), bf16),
                 pltpu.VMEM((2, CELLS, width), f32),
                 pltpu.VMEM((2, WIDE, width), bf16),
                 pltpu.VMEM((2, 2 * EDGE, width), bf16),

time: 164 us -> 164 us (level)
  no operation moved by 1% of the time
where the time goes in v1:
time: 164 us
  Pallas kernels  154 us (94%)
  between operations  5.39 us (3%)
  other arithmetic  2.96 us (2%)
    pallas_call x1, Pallas kernels, shards(): lax.switch(lengths[0] // 4 + 2 * (lengths[1] // 4), [run(which) for which...  154 us

profile of v1, /device:TPU:33, one launch (start us, length us, event | category | flops | bytes accessed | tf_op | source)
XLA Modules:
  0.0 164.2 jit_solution(6633779661460635224)
XLA Ops:
  0.0 0.1 pad.2.clone
  0.1 0.7 convert_element_type.3
  0.8 0.7 broadcast_multiply_fusion
  1.4 0.1 maximum_maximum_fusion
  1.5 1.5 slice_reduce_fusion
  8.4 154.4 %conditional.1 = (f32[1,4,2,6,24,512]{5,4,3,2,1,0:T(8,128)S(1)}) conditional(s32[]{:T(128)} %clamp.3, (s32[4]{0:T(128)}, bf16[4,2,6,24,512]{4,3,2,1,0:T(8,128)(2,1)}, f32[2,128]{1,0:T(2,128)S(1)}, f32[2,2,512]{2,1,0:T(2,128)}, bf16[2,512,1536]{2,1,0:T(8,128)(2,1)}, /*index=5*/bf16[2,512,512]{2,1,0:T(8,128)(2,1)}, ...), branch_computations={%region_2.3_spmd.clone, %region_3.4_spmd.clone, %region_4.5_spmd.c... | conditional | flops 32000000000 | bytes 20000008 | solution.py:550
  8.4 154.1 %branch_0_fun.1 = f32[4,288,512]{2,1,0:T(8,128)S(1)} custom-call(s32[4]{0:T(128)} %get-tuple-element.140.depth_ref, bf16[4,288,512]{2,1,0:T(8,128)(2,1)} %bitcast.15, f32[2,1,128]{2,1,0:T(1,128)S(1)} %bitcast.12, f32[2,2,512]{2,1,0:T(2,128)} %get-tuple-element.142.gains_in, f32[288,128]{1,0:T(8,128)} %constant.31.clone.4.table, ...), custom_call_target="tpu_custom_call" | custom-call | flops 32000000000 | bytes 20000000 | tf_op jit(solution)/shard_map/cond/branch_0_fun/pallas_call | solution.py:550
  162.8 1.4 copy.63
  (1 shorter events, 0.0 us)

commit v2 on v1

--- a/solution.py
+++ b/solution.py
@@ -33,7 +33,8 @@
             for lon in range(2):
                 which = core * 8 + lat * 2 + lon
                 for at in range(CELLS):
-                    window, half, pair, cell = at // 144, at % 144 // 72, at % 72 // 36, at % 36
+                    window = at // 144 if core else 1 - at // 144
+                    half, pair, cell = at % 144 // 72, at % 72 // 36, at % 36
                     level, row, column = cell // 18, cell % 18 // 6, cell % 6
                     column += (2 * window + pair) * 6 + lon * (6 - 12 * core)
                     across = column >= 24 or column < 0
@@ -63,7 +64,7 @@
                     elif across:
                         take = AT_LON + source * EDGE + inside - source * 64 - (0 if core else 32)
                     else:
-                        take = window * 144 + inside
+                        take = (window if core else 1 - window) * 144 + inside
                     table[at, which + 4] = take
     return table
 
@@ -182,13 +183,13 @@
     def forth(b):
         return edges(
             (
+                (packed.at[b, rows_from(EDGE * core, EDGE)], src.at[b, pl.ds(AT_BOTH, EDGE)], to_nw),
+                (packed.at[b], src.at[b, pl.ds(AT_LON, 2 * EDGE)], to_w),
                 (src.at[b, rows_from(64 * core, REACH)], src.at[b, pl.ds(AT_LAT, REACH)], to_n),
                 (
                     src.at[b, rows_from(HALF + 64 * core, REACH)],
                     src.at[b, pl.ds(AT_LAT + REACH, REACH)], to_n,
                 ),
-                (packed.at[b], src.at[b, pl.ds(AT_LON, 2 * EDGE)], to_w),
-                (packed.at[b, rows_from(EDGE * core, EDGE)], src.at[b, pl.ds(AT_BOTH, EDGE)], to_nw),
             ),
             f_send.at[b], f_recv.at[b],
         )
@@ -196,17 +197,17 @@
     def back(b):
         return edges(
             (
+                (ret.at[b, rows_from(96 - 96 * core, EDGE)], ret.at[b, pl.ds(AT_BOTH, EDGE)], to_se),
+                (ret.at[b, rows_from(32 - 32 * core, EDGE)], ret.at[b, pl.ds(AT_LON, EDGE)], to_e),
+                (
+                    ret.at[b, rows_from(96 - 32 * core, EDGE)],
+                    ret.at[b, pl.ds(AT_LON + EDGE, EDGE)], to_e,
+                ),
                 (ret.at[b, rows_from(64 - 64 * core, REACH)], ret.at[b, pl.ds(AT_LAT, REACH)], to_s),
                 (
                     ret.at[b, rows_from(208 - 64 * core, REACH)],
                     ret.at[b, pl.ds(AT_LAT + REACH, REACH)], to_s,
                 ),
-                (ret.at[b, rows_from(176 - 176 * core, EDGE)], ret.at[b, pl.ds(AT_LON, EDGE)], to_e),
-                (
-                    ret.at[b, rows_from(240 - 176 * core, EDGE)],
-                    ret.at[b, pl.ds(AT_LON + EDGE, EDGE)], to_e,
-                ),
-                (ret.at[b, rows_from(240 - 240 * core, EDGE)], ret.at[b, pl.ds(AT_BOTH, EDGE)], to_se),
             ),
             b_send.at[b], b_recv.at[b],
         )
@@ -350,14 +351,17 @@
         replace_rows(src, b, l, core)
         cells = dot(fwd[step], src[b, 0:TAKEN]).astype(jnp.bfloat16)
         bias = small[l, 0:1, 0:1] * cross[...]
-        done = [[], []]
+        quads = []
         for g in range(2):
             lanes = [slice(p * 512 + g * 256, p * 512 + g * 256 + 256) for p in range(3)]
             q = unit(dot(cells, weight(0, lanes[0])))
             k = unit(dot(cells, weight(0, lanes[1])))
-            v = dot(cells, weight(0, lanes[2])).astype(jnp.bfloat16)
-            for w in range(2):
-                part = slice(w * HALF, w * HALF + HALF)
+            quads.append((q, k, dot(cells, weight(0, lanes[2])).astype(jnp.bfloat16)))
+        copies = back(b)
+        for w in range(2):
+            part = slice(w * HALF, w * HALF + HALF)
+            done = []
+            for g, (q, k, v) in enumerate(quads):
                 heads = jnp.concatenate([q[part] * masks[h] for h in range(4)], axis=0)
                 scores = lax.dot_general(
                     heads, k[part], (((1,), (1,)), ((), ())), preferred_element_type=jnp.float32
@@ -376,11 +380,10 @@
                     at = slice(p * 128, p * 128 + 128)
                     one = mixed[2 * p * HALF : (2 * p + 1) * HALF, at] * shares[2 * p]
                     two = mixed[(2 * p + 1) * HALF : (2 * p + 2) * HALF, at] * shares[2 * p + 1]
-                    done[w].append(jnp.where(first_of_pair, one, two).astype(jnp.bfloat16))
-        for w in range(2):
-            ret[b, w * HALF : w * HALF + HALF] = jnp.concatenate(done[w], axis=1)
-        for copy in back(b):
-            copy.start()
+                    done.append(jnp.where(first_of_pair, one, two).astype(jnp.bfloat16))
+            ret[b, part] = jnp.concatenate(done, axis=1)
+            for copy in copies[:3] if w == 0 else copies[3:]:
+                copy.start()
 
     def feed(b, step, l, weight):
         for copy in back(b):

time: 164 us -> 138 us (0.84)
  Pallas kernels: 154 us -> 128 us
    pallas_call x1, Pallas kernels: 154 us -> 128 us  [shards(): lax.switch(lengths[0] // 4 + 2 * (lengths[1] // 4), [run(which) for which...]
where the time goes in v2:
time: 138 us
  Pallas kernels  128 us (93%)
  between operations  5.39 us (4%)
  other arithmetic  2.96 us (2%)
  local copies, waits for them, and re-layouts  1.49 us (1%)
    pallas_call x1, Pallas kernels, shards(): lax.switch(lengths[0] // 4 + 2 * (lengths[1] // 4), [run(which) for which...  128 us

profile of v2, /device:TPU:33, one launch (start us, length us, event | category | flops | bytes accessed | tf_op | source)
XLA Modules:
  0.0 137.8 jit_solution(9881013457304907039)
XLA Ops:
  0.0 0.1 pad.2.clone
  0.1 0.7 convert_element_type.3
  0.8 0.7 broadcast_multiply_fusion
  1.4 0.1 maximum_maximum_fusion
  1.5 1.5 %slice_reduce_fusion = (s32[]{:T(128)}, s32[]{:T(128)}) fusion(s32[4]{0:T(128)} %param.14), kind=kLoop, calls=%fused_computation.2 | loop fusion | flops 2 | bytes 24 | tf_op jit(solution)/shard_map/reduce_sum | solution.py:552
  8.4 128.0 %conditional.1 = (f32[1,4,2,6,24,512]{5,4,3,2,1,0:T(8,128)S(1)}) conditional(s32[]{:T(128)} %clamp.3, (s32[4]{0:T(128)}, bf16[4,2,6,24,512]{4,3,2,1,0:T(8,128)(2,1)}, f32[2,128]{1,0:T(2,128)S(1)}, f32[2,2,512]{2,1,0:T(2,128)}, bf16[2,512,1536]{2,1,0:T(8,128)(2,1)}, /*index=5*/bf16[2,512,512]{2,1,0:T(8,128)(2,1)}, ...), branch_computations={%region_2.3_spmd.clone, %region_3.4_spmd.clone, %region_4.5_spmd.c... | conditional | flops 32000000000 | bytes 20000008 | solution.py:553
  8.4 127.7 %branch_0_fun.1 = f32[4,288,512]{2,1,0:T(8,128)S(1)} custom-call(s32[4]{0:T(128)} %get-tuple-element.140.depth_ref, bf16[4,288,512]{2,1,0:T(8,128)(2,1)} %bitcast.15, f32[2,1,128]{2,1,0:T(1,128)S(1)} %bitcast.12, f32[2,2,512]{2,1,0:T(2,128)} %get-tuple-element.142.gains_in, f32[288,128]{1,0:T(8,128)} %constant.31.clone.4.table, ...), custom_call_target="tpu_custom_call" | custom-call | flops 32000000000 | bytes 20000000 | tf_op jit(solution)/shard_map/cond/branch_0_fun/pallas_call | solution.py:553
  136.4 1.4 %copy.63 = f32[1,4,2,6,24,512]{5,4,3,2,1,0:T(8,128)} copy(f32[1,4,2,6,24,512]{5,4,3,2,1,0:T(8,128)S(1)} %get-tuple-element.91) | data formatting | bytes 4718592
  (1 shorter events, 0.0 us)
